TPU v7x, 32 devices: a whole 2x2x4 slice. The times are simulated.
32 devices in a mesh: sector: 4 (over y, core), term: 8 (over z, x).
Axes of the slice: x: 2, y: 2, z: 4, core: 2. Of those that a mesh axis runs over, the one named last changes fastest.
Arguments:
- trial: float32 [8, 512, 512], P('sector', 'term'), may hold values from -6 to 6
- precond: float32 [8, 512, 512], P('sector', 'term'), may hold values from 2 to 16
- sector_dims: int32 [8], P('sector'), may hold values from 128 to 512
- left_ops: float32 [256, 512, 512], P(('sector', 'term')), may hold values from -0.25 to 0.25
- right_ops: float32 [256, 512, 512], P(('sector', 'term')), may hold values from -0.25 to 0.25
- task_source: int32 [256], P(('sector', 'term')), may hold values from 0 to 1
- task_target: int32 [256], P(('sector', 'term')), may hold values from 0 to 1
- task_count: int32 [32], P(('sector', 'term')), may hold values from 1 to 7, as said below
Outputs:
- trial_out: float32 [8, 512, 512], P('sector', 'term')
- ritz: float32 [3], replicated
Inputs may be any that keep to these rules, and one draw needn't show every extreme that they name: `task_count`: the counts of two devices with the same sector index whose term indices differ by half the term axis add up to 8.
All inputs are finite; a program needn't handle non-finite values.
Results may differ from a plain program's by a relative error of at most 0.0003.
Values sent between devices are 32-bit elements; how exact they have to be, the bound alone decides.
No kernel may reach another device: no remote copies, remote signals or barrier semaphores. Data moves between devices by JAX's collectives and lax.ppermute only.
A program may use at most 64 MiB of HBM per device.

v0:
```python
import functools

import jax
import jax.numpy as jnp
from jax import lax
from jax.experimental import pallas as pl
from jax.experimental.pallas import tpu as pltpu
from jax.sharding import PartitionSpec as P

STEPS = 3
VMEM_LIMIT = 14 * 1024 * 1024
F32 = jnp.float32
BF16 = jnp.bfloat16


def split(value):
    high = value.astype(BF16)
    return high, (value - high.astype(F32)).astype(BF16)


def dot3(a_high, a_low, b_high, b_low):
    def dot(a, b):
        return jnp.dot(a, b, preferred_element_type=F32)

    return dot(a_high, b_high) + (dot(a_high, b_low) + dot(a_low, b_high))


def call(kernel, name, info, arrays, results, flops, scratch=()):
    held = pl.BlockSpec(memory_space=pltpu.VMEM)
    return pl.pallas_call(
        kernel,
        in_specs=[pl.BlockSpec(memory_space=pltpu.SMEM)] + [held] * len(arrays),
        out_specs=[held] * len(results),
        out_shape=[pltpu.VMEM(shape, dtype) for shape, dtype in results],
        scratch_shapes=list(scratch),
        compiler_params=pltpu.CompilerParams(vmem_limit_bytes=VMEM_LIMIT),
        cost_estimate=pl.CostEstimate(flops=flops, bytes_accessed=0, transcendentals=0),
        name=name,
    )(info, *arrays)


class Place:
    def __init__(self, slots):
        self.target, self.ring, self.side = slots, 2 * slots, 2 * slots + 1
        self.count, self.limits = 2 * slots + 2, 2 * slots + 3


def split_kernel(at, info, operator, *refs):
    high, low = refs[-2:]
    k = pl.program_id(0)

    @pl.when(k < info[at.count])
    def _():
        high[k], low[k] = split(operator[0])


def split_operators(info, operators, earlier, name):
    slots, width, _ = operators.shape
    at = Place(slots)
    return pl.pallas_call(
        functools.partial(split_kernel, at),
        grid_spec=pltpu.PrefetchScalarGridSpec(
            num_scalar_prefetch=1,
            grid=(slots - 1,),
            in_specs=[
                pl.BlockSpec(
                    (1, width, width), lambda k, info: (jnp.minimum(k, info[at.count] - 1), 0, 0)
                )
            ]
            + [pl.BlockSpec(memory_space=pltpu.VMEM)] * len(earlier),
            out_specs=[pl.BlockSpec(memory_space=pltpu.VMEM)] * 2,
        ),
        out_shape=[pltpu.VMEM((slots - 1, width, width), BF16)] * 2,
        compiler_params=pltpu.CompilerParams(vmem_limit_bytes=VMEM_LIMIT),
        cost_estimate=pl.CostEstimate(
            flops=0, bytes_accessed=slots * width * width * 4, transcendentals=0
        ),
        name=name,
    )(info, operators, *earlier)


def split_blocks(blocks, high, low):
    share = blocks[0].shape[1]
    for place, block in enumerate(blocks):
        rows = pl.ds(place * share, share)
        high[:, rows, :], low[:, rows, :] = split(block[...])


def lanes(value):
    total = jnp.sum(value, axis=tuple(range(value.ndim - 1)))[None]
    width = total.shape[1]
    return sum(total[:, c : c + 128] for c in range(0, width, 128))


def inner_kernel(at, ring, info, *refs):
    blocks = refs[:ring]
    right_high, right_low = refs[ring : ring + 2]
    out_high, out_low, token, high, low = refs[-5:]
    token[...] = jnp.zeros_like(token)
    split_blocks(blocks, high, low)

    def one(k, carry):
        source = info[k]
        out_high[k], out_low[k] = split(
            dot3(high[source], low[source], right_high[k], right_low[k])
        )
        return carry

    lax.fori_loop(0, info[at.count], one, 0)


def inner_rows(at, info, blocks, right, earlier=()):
    ring = len(blocks)
    live, width, _ = right[0].shape
    sectors, share, _ = blocks[0].shape
    rows = ring * share
    return call(
        functools.partial(inner_kernel, at, ring),
        "inner_rows",
        info,
        [*blocks, *right, *earlier],
        [((live, rows, width), BF16)] * 2 + [((1, 128), F32)],
        live * rows * width * width * 6,
        [pltpu.VMEM((sectors, rows, width), BF16)] * 2,
    )


def first_row(at, info, ring, share, offset, side):
    around = lax.rem(info[at.ring] + offset, ring)
    return pl.multiple_of((around * 2 + side) * share, share)


def outer_rows(at, info, k, ring, places, left, full, outs):
    share = outs[0].shape[1]
    picks = [pl.ds(first_row(at, info, ring, share, *place), share) for place in places]
    high, low = (
        jnp.concatenate([part[k, pick, :] for pick in picks], axis=0) for part in left
    )
    product = dot3(high, low, full[0][k], full[1][k])
    target = info[at.target + k]
    for i, out in enumerate(outs):
        out[target] += product[i * share : (i + 1) * share]


def middle_kernel(at, ring, last, groups, order, head, info, *refs):
    block, parts, refs = refs[0], refs[1 : 1 + 2 * len(groups)], refs[1 + 2 * len(groups) :]
    right_high, right_low, left_high, left_low = refs[:4]
    full_high, full_low = refs[4:6]
    outs, (high, low) = refs[6:-2], refs[-2:]
    share = block.shape[1]
    side = info[at.side]
    split_blocks([block], high, low)
    for out in outs:
        out[...] = jnp.zeros_like(out)
    places = [(r, 1 - side) for r in order[: head[0]]] + [(r, side) for r in order[: head[1]]]

    def put(out, k, r, other, value):
        rows = pl.ds(first_row(at, info, ring, share, r, 1 - side if other else side), share)
        out[k, rows, :] = value

    def one(k, carry):
        source = info[k]
        inner = split(dot3(high[source], low[source], right_high[k], right_low[k]))
        for which, out in enumerate((full_high, full_low)):
            for g, group in enumerate(groups):
                for i, (r, other) in enumerate(group):
                    put(out, k, r, other, parts[2 * g + which][k, i * share : (i + 1) * share, :])
            put(out, k, last, True, inner[which])
        outer_rows(
            at, info, k, ring, places, (left_high, left_low), (full_high, full_low), outs
        )
        return carry

    lax.fori_loop(0, info[at.count], one, 0)


def middle(at, info, ring, last, groups, order, head, block, parts, right, left):
    live, width, _ = right[0].shape
    sectors, share, _ = block.shape
    count = sum(head)
    results = call(
        functools.partial(middle_kernel, at, ring, last, groups, order, head),
        "middle",
        info,
        [block, *(array for part in parts for array in part), *right, *left],
        [((live, width, width), BF16)] * 2 + [(block.shape, F32)] * count,
        live * share * (1 + count) * width * width * 6,
        [pltpu.VMEM((sectors, share, width), BF16)] * 2,
    )
    return results[:2], results[2 : 2 + head[0]], results[2 + head[0] :]


def tail_kernel(at, ring, order, head, info, *refs):
    mine, theirs, refs = refs[:ring], refs[ring : 2 * ring], refs[2 * ring :]
    heads, refs = refs[: sum(head)], refs[sum(head) :]
    full_high, full_low, left_high, left_low, squares, sums = refs[:6]
    outs = refs[6:]
    side = info[at.side]
    for out in outs:
        out[...] = jnp.zeros_like(out)
    others, owns = order[head[0] :], order[head[1] :]
    places = [(r, 1 - side) for r in others] + [(r, side) for r in owns]

    def one(k, carry):
        outer_rows(
            at, info, k, ring, places, (left_high, left_low), (full_high, full_low), outs
        )
        return carry

    lax.fori_loop(0, info[at.count], one, 0)
    pairs = [(theirs[r], heads[i]) for i, r in enumerate(order[: head[0]])]
    pairs += [(mine[r], heads[head[0] + i]) for i, r in enumerate(order[: head[1]])]
    pairs += [(theirs[r], outs[i]) for i, r in enumerate(others)]
    pairs += [(mine[r], outs[len(others) + i]) for i, r in enumerate(owns)]
    dots = sum(lanes(block[...] * out[...]) for block, out in pairs)
    row = lax.broadcasted_iota(jnp.int32, sums.shape, 0)
    sums[...] = jnp.where(row == 0, dots, jnp.where(row == 1, squares[...], 0.0))


def tail(at, info, ring, order, head, mine, theirs, heads, full, left, squares):
    live, width, _ = left[0].shape
    share = mine[0].shape[1]
    count = 2 * ring - sum(head)
    results = call(
        functools.partial(tail_kernel, at, ring, order, head),
        "tail",
        info,
        [*mine, *theirs, *heads, *full, *left, squares],
        [((8, 128), F32)] + [(mine[0].shape, F32)] * count,
        0,
    )
    others = ring - head[0]
    return results[0], results[1 : 1 + others], results[1 + others :]


def inside(at, info, shape, ring):
    share = shape[1]
    start = (info[at.ring] * 2 + info[at.side]) * share
    rows = start + lax.broadcasted_iota(jnp.int32, shape[1:], 0)
    cols = lax.broadcasted_iota(jnp.int32, shape[1:], 1)
    return [
        ((rows < info[at.limits + s]) & (cols < info[at.limits + s])).astype(F32)
        for s in range(shape[0])
    ]


def begin_kernel(at, ring, info, trial, vector, squares):
    total = jnp.zeros(squares.shape, F32)
    for s, mask in enumerate(inside(at, info, trial.shape, ring)):
        value = mask * trial[s]
        vector[s] = value
        total = total + lanes(value * value)
    squares[...] = total


def begin(at, info, trial, ring):
    return call(
        functools.partial(begin_kernel, at, ring),
        "begin",
        info,
        [trial],
        [(trial.shape, F32), ((1, 128), F32)],
        trial.size * 4,
    )


def update_kernel(at, ring, info, *refs):
    vector, precond, refs = refs[0], refs[1], refs[2:]
    sums, terms, (result, squares, ritz) = refs[:ring], refs[ring:-3], refs[-3:]
    sums = [part[...] for part in sums]
    while len(sums) > 1:
        half = len(sums) // 2
        sums = [sums[r] + sums[r + half] for r in range(half)]
    both = jnp.sum(sums[0], axis=1, keepdims=True)
    theta = both[0:1] / both[1:2]
    ritz[...] = jnp.broadcast_to(theta, ritz.shape)
    total = jnp.zeros(squares.shape, F32)
    for s, mask in enumerate(inside(at, info, vector.shape, ring)):
        sig = mask * sum(term[s] for term in terms)
        value = vector[s] - (sig - theta * vector[s]) / precond[s]
        result[s] = value
        total = total + lanes(value * value)
    squares[...] = total


def update(at, info, vector, precond, sums, terms, ring):
    return call(
        functools.partial(update_kernel, at, ring),
        "update",
        info,
        [vector, precond, *sums, *terms],
        [(vector.shape, F32), ((1, 128), F32), ((1, 128), F32)],
        vector.size * 8,
    )


def across(value, terms):
    return lax.ppermute(value, "term", [(i, i ^ 1) for i in range(terms)])


def around(value, terms, shift):
    return lax.ppermute(value, "term", [(i, (i + 2 * shift) % terms) for i in range(terms)])


def stages(sectors, terms):
    inner = [("term", terms, 1)]
    across_sectors = [("sector", sectors, 1 << bit) for bit in range(sectors.bit_length() - 1)]
    outer = [("term", terms, 1 << bit) for bit in range(1, terms.bit_length() - 1)]
    return inner + across_sectors, outer


def stage_sum(values, stage):
    axis, size, step = stage
    return values + lax.ppermute(values, axis, [(i, i ^ step) for i in range(size)])


def send_order(ring):
    ups = ring // 2
    downs = ring - 1 - ups
    order = []
    for hop in range(ups, 0, -1):
        order.append(hop)
        if hop <= downs:
            order.append((ring - hop) % ring)
    return order + [0]


def scatter_sum(own, other, terms, sums, steps):
    ring = terms // 2
    ups = ring // 2
    downs = ring - 1 - ups
    received = {r: across(other[r], terms) for r in send_order(ring)}
    inner, *outer = steps
    sums = stage_sum(sums, inner)
    up = down = None
    for hop in range(ups, 0, -1):
        value = own[hop] + received[hop]
        value, sums = lax.optimization_barrier((value if up is None else value + up, sums))
        up = around(value, terms, 1)
        if hop == ups:
            for stage in outer:
                sums = stage_sum(sums, stage)
        if hop <= downs:
            back = (ring - hop) % ring
            value = own[back] + received[back]
            value, sums = lax.optimization_barrier((value if down is None else value + down, sums))
            down = around(value, terms, -1)
    parts = [sums] + [around(sums, terms, shift) for shift in range(1, ring)]
    return [term for term in (own[0], received[0], up, down) if term is not None], parts


def per_device(
    trial, precond, sector_dims, left_ops, right_ops, task_source, task_target, task_count
):
    sec_dev, share, width = trial.shape
    slots = left_ops.shape[0]
    sectors, terms = lax.axis_size("sector"), lax.axis_size("term")
    ring = terms // 2
    cells = float(sec_dev * sectors * width * width)
    term = lax.axis_index("term").astype(jnp.int32)
    at = Place(slots)
    info = jnp.concatenate(
        [task_source, task_target, jnp.stack([term // 2, term % 2]), task_count, sector_dims]
    )
    values = []
    vector, squares = begin(at, info, trial, ring)
    steps, outer_steps = stages(sectors, terms)
    order = send_order(ring)
    ups = ring // 2
    downs = ring - 1 - ups
    last = ring - ups
    head = (ring // 2, ring // 4)
    right = left = None
    for step in range(STEPS):
        mine, theirs, groups, parts = {0: vector}, {}, [], []
        token = None
        for hop in range(1, ups + 1):
            value = mine[(ring - hop + 1) % ring]
            if token is not None:
                value, token = lax.optimization_barrier((value, token))
                if step == 0 and hop == 2:
                    theirs[0], token = token, None
            mine[ring - hop] = around(value, terms, 1)
            fresh = [(ring - hop + 1) % ring]
            if hop <= downs:
                mine[hop] = around(mine[hop - 1], terms, -1)
            if hop > 1 and hop - 1 <= downs:
                fresh.append(hop - 1)
            for r in fresh:
                theirs[r] = across(mine[r], terms)
            if step == 0 and hop == 1:
                token = theirs[0]
                continue
            if step == 0 and hop == 2:
                arrived = [mine[ring - 1], mine[1]]
                right = split_operators(info, right_ops, arrived, "split_right")
                left = split_operators(info, left_ops, arrived, "split_left")
                group = [(0, False), (0, True)] + [(r, False) for r in fresh]
            elif hop == 1:
                group = [(0, False), (0, True)]
            else:
                group = [(r, False) for r in fresh] + before
            before = [(r, True) for r in fresh]
            if hop == 1:
                before = []
            *part, token = inner_rows(
                at,
                info,
                [(theirs if other else mine)[r] for r, other in group],
                right,
                () if token is None else (token,),
            )
            groups.append(group)
            parts.append(part)
        fresh = [last] + ([ups] if ups <= downs else [])
        for r in fresh:
            theirs[r] = across(mine[r], terms)
        group = [(r, False) for r in fresh] + before + [(r, True) for r in fresh if r != last]
        *part, token = inner_rows(
            at, info, [(theirs if other else mine)[r] for r, other in group], right, (token,)
        )
        groups.append(group)
        parts.append(part)
        full, others, owns = middle(
            at, info, ring, last, groups, order, head, theirs[last], parts, right, left
        )
        sums, more_others, more_owns = tail(
            at,
            info,
            ring,
            order,
            head,
            [mine[r] for r in range(ring)],
            [theirs[r] for r in range(ring)],
            [*others, *owns],
            full,
            left,
            squares,
        )
        others = dict(zip(order, [*others, *more_others]))
        owns = dict(zip(order, [*owns, *more_owns]))
        summed, sums = scatter_sum(owns, others, terms, sums, steps)
        vector, squares, ritz = update(at, info, vector, precond, sums, summed, ring)
        values.append(ritz[0, :1])
    for stage in steps + outer_steps:
        squares = stage_sum(squares, stage)
    return (vector * jnp.sqrt(cells / jnp.sum(squares)), jnp.concatenate(values))


def solution(mesh):
    return jax.shard_map(
        per_device,
        mesh=mesh,
        in_specs=(
            P("sector", "term", None),
            P("sector", "term", None),
            P("sector"),
            P(("sector", "term"), None, None),
            P(("sector", "term"), None, None),
            P(("sector", "term")),
            P(("sector", "term")),
            P(("sector", "term")),
        ),
        out_specs=(P("sector", "term", None), P()),
        check_vma=False,
    )
```

profile of v0, /device:TPU:0, one launch (start us, length us, event | category | flops | bytes accessed | tf_op | source)
XLA Modules:
  0.0 244.9 jit_solution(213491612069880444)
XLA Ops:
  12.9 4.8 %collective-permute-done.1.refs_0_.refs_2_.refs_3_ = f32[2,64,512]{2,1,0:T(8,128)S(1)} collective-permute-done((f32[2,64,512]{2,1,0:T(8,128)S(1)}, f32[2,64,512]{2,1,0:T(8,128)S(1)}, u32[]{:S(2)}, u32[]{:S(2)}) %collective-permute-start.1) | collective-permute-done | bytes 262176 | tf_op jit(solution)/shard_map/ppermute | solution.py:302
  18.0 4.1 %collective-permute-done.refs_1_.refs_3_ = f32[2,64,512]{2,1,0:T(8,128)S(1)} collective-permute-done((f32[2,64,512]{2,1,0:T(8,128)S(1)}, f32[2,64,512]{2,1,0:T(8,128)S(1)}, u32[]{:S(2)}, u32[]{:S(2)}) %collective-permute-start) | collective-permute-done | bytes 262176 | tf_op jit(solution)/shard_map/ppermute | solution.py:302
  29.1 4.8 %inner_rows.8 = (bf16[7,256,512]{2,1,0:T(8,128)(2,1)S(1)}, bf16[7,256,512]{2,1,0:T(8,128)(2,1)S(1)}, f32[1,128]{1,0:T(1,128)S(1)}) custom-call(s32[21]{0:T(128)S(1)} %concatenate.6.info, f32[2,64,512]{2,1,0:T(8,128)S(1)} %get-tuple-element.95.refs_0_, f32[2,64,512]{2,1,0:T(8,128)S(1)} %collective-permute-done.2.refs_1_.refs_4_, ...), custom_call_target="tpu_custom_call" | custom-call | flops 2818572288 | tf_op jit(solution)/shard_map/inner_rows/pallas_call | solution.py:30
  35.7 4.6 %inner_rows.9 = (bf16[7,192,512]{2,1,0:T(8,128)(2,1)S(1)}, bf16[7,192,512]{2,1,0:T(8,128)(2,1)S(1)}, f32[1,128]{1,0:T(1,128)}) custom-call(s32[21]{0:T(128)S(1)} %concatenate.6.info, f32[2,64,512]{2,1,0:T(8,128)S(1)} %collective-permute-done.3.refs_0_.refs_2_, f32[2,64,512]{2,1,0:T(8,128)S(1)} %collective-permute-done.6.refs_1_.refs_7_, ...), custom_call_target="tpu_custom_call" | custom-call | flops 2113929216 | tf_op jit(solution)/shard_map/inner_rows/pallas_call | solution.py:30
  40.2 6.7 %middle.3 = (bf16[7,512,512]{2,1,0:T(8,128)(2,1)S(1)}, bf16[7,512,512]{2,1,0:T(8,128)(2,1)S(1)}, f32[2,64,512]{2,1,0:T(8,128)S(1)}, f32[2,64,512]{2,1,0:T(8,128)S(1)}, f32[2,64,512]{2,1,0:T(8,128)S(1)}) custom-call(s32[21]{0:T(128)S(1)} %concatenate.6.info, f32[2,64,512]{2,1,0:T(8,128)S(1)} %collective-permute-done.5.refs_0_.refs_6_, ...), custom_call_target="tpu_custom_call" | custom-call | flops 2818572288 | tf_op jit(solution)/shard_map/middle/pallas_call | solution.py:30
  47.1 5.6 %tail.3 = (f32[8,128]{1,0:T(8,128)S(1)}, f32[2,64,512]{2,1,0:T(8,128)S(1)}, f32[2,64,512]{2,1,0:T(8,128)S(1)}, f32[2,64,512]{2,1,0:T(8,128)S(1)}, f32[2,64,512]{2,1,0:T(8,128)S(1)}, /*index=5*/f32[2,64,512]{2,1,0:T(8,128)S(1)}) custom-call(s32[21]{0:T(128)S(1)} %concatenate.6.info, f32[2,64,512]{2,1,0:T(8,128)S(1)} %get-tuple-element.95.refs_0_, ...), custom_call_target="tpu_custom_call" | custom-call | tf_op jit(solution)/shard_map/tail/pallas_call | solution.py:30
  59.2 6.7 %collective-permute-done.7 = f32[2,64,512]{2,1,0:T(8,128)S(1)} collective-permute-done((f32[2,64,512]{2,1,0:T(8,128)S(1)}, f32[2,64,512]{2,1,0:T(8,128)S(1)}, u32[]{:S(2)}, u32[]{:S(2)}) %collective-permute-start.7) | collective-permute-done | bytes 262176 | tf_op jit(solution)/shard_map/ppermute | solution.py:298
  70.6 10.3 %collective-permute-done.16.refs_5_ = f32[8,128]{1,0:T(8,128)S(1)} collective-permute-done((f32[8,128]{1,0:T(8,128)S(1)}, f32[8,128]{1,0:T(8,128)S(1)}, u32[]{:S(2)}, u32[]{:S(2)}) %collective-permute-start.16) | collective-permute-done | bytes 4128 | tf_op jit(solution)/shard_map/ppermute | solution.py:302
  82.1 3.7 %collective-permute-start.20 = (f32[2,64,512]{2,1,0:T(8,128)S(1)}, f32[2,64,512]{2,1,0:T(8,128)S(1)}, u32[]{:S(2)}, u32[]{:S(2)}) collective-permute-start(f32[2,64,512]{2,1,0:T(8,128)S(1)} %get-tuple-element.125.refs_0_), channel_id=1, source_target_pairs={{0,6},{1,7},{2,0},{3,1},{4,2},{5,3},{6,4},{7,5},{8,14},{9,15},{10,... | collective-permute-start | bytes 786440 | tf_op jit(solution)/shard_map/ppermute | solution.py:302
  85.8 4.3 %collective-permute-done.22.refs_1_.refs_4_ = f32[2,64,512]{2,1,0:T(8,128)S(1)} collective-permute-done((f32[2,64,512]{2,1,0:T(8,128)S(1)}, f32[2,64,512]{2,1,0:T(8,128)S(1)}, u32[]{:S(2)}, u32[]{:S(2)}) %collective-permute-start.22) | collective-permute-done | bytes 262176 | tf_op jit(solution)/shard_map/ppermute | solution.py:298
  97.5 5.8 %collective-permute-done.23.refs_0_.refs_2_ = f32[2,64,512]{2,1,0:T(8,128)S(1)} collective-permute-done((f32[2,64,512]{2,1,0:T(8,128)S(1)}, f32[2,64,512]{2,1,0:T(8,128)S(1)}, u32[]{:S(2)}, u32[]{:S(2)}) %collective-permute-start.23) | collective-permute-done | bytes 262176 | tf_op jit(solution)/shard_map/ppermute | solution.py:302
  108.3 4.6 %inner_rows.12 = (bf16[7,192,512]{2,1,0:T(8,128)(2,1)S(1)}, bf16[7,192,512]{2,1,0:T(8,128)(2,1)S(1)}, f32[1,128]{1,0:T(1,128)}) custom-call(s32[21]{0:T(128)S(1)} %concatenate.6.info, f32[2,64,512]{2,1,0:T(8,128)S(1)} %collective-permute-done.23.refs_0_.refs_2_, f32[2,64,512]{2,1,0:T(8,128)S(1)} %collective-permute-done.26.refs_1_.refs_7_, ...), custom_call_target="tpu_custom_call" | custom-call | flops 2113929216 | tf_op jit(solution)/shard_map/inner_rows/pallas_call | solution.py:30
  112.9 6.8 %middle.4 = (bf16[7,512,512]{2,1,0:T(8,128)(2,1)S(1)}, bf16[7,512,512]{2,1,0:T(8,128)(2,1)S(1)}, f32[2,64,512]{2,1,0:T(8,128)S(1)}, f32[2,64,512]{2,1,0:T(8,128)S(1)}, f32[2,64,512]{2,1,0:T(8,128)S(1)}) custom-call(s32[21]{0:T(128)S(1)} %concatenate.6.info, f32[2,64,512]{2,1,0:T(8,128)S(1)} %collective-permute-done.25.refs_0_.refs_6_, ...), custom_call_target="tpu_custom_call" | custom-call | flops 2818572288 | tf_op jit(solution)/shard_map/middle/pallas_call | solution.py:30
  119.7 5.6 %tail.4 = (f32[8,128]{1,0:T(8,128)S(1)}, f32[2,64,512]{2,1,0:T(8,128)S(1)}, f32[2,64,512]{2,1,0:T(8,128)S(1)}, f32[2,64,512]{2,1,0:T(8,128)S(1)}, f32[2,64,512]{2,1,0:T(8,128)S(1)}, /*index=5*/f32[2,64,512]{2,1,0:T(8,128)S(1)}) custom-call(s32[21]{0:T(128)S(1)} %concatenate.6.info, f32[2,64,512]{2,1,0:T(8,128)S(1)} %get-tuple-element.125.refs_0_, ...), custom_call_target="tpu_custom_call" | custom-call | tf_op jit(solution)/shard_map/tail/pallas_call | solution.py:30
  131.8 8.4 %collective-permute-done.27 = f32[2,64,512]{2,1,0:T(8,128)S(1)} collective-permute-done((f32[2,64,512]{2,1,0:T(8,128)S(1)}, f32[2,64,512]{2,1,0:T(8,128)S(1)}, u32[]{:S(2)}, u32[]{:S(2)}) %collective-permute-start.27) | collective-permute-done | bytes 262176 | tf_op jit(solution)/shard_map/ppermute | solution.py:298
  144.9 7.9 %collective-permute-done.36.refs_5_ = f32[8,128]{1,0:T(8,128)S(1)} collective-permute-done((f32[8,128]{1,0:T(8,128)S(1)}, f32[8,128]{1,0:T(8,128)S(1)}, u32[]{:S(2)}, u32[]{:S(2)}) %collective-permute-start.36) | collective-permute-done | bytes 4128 | tf_op jit(solution)/shard_map/ppermute | solution.py:302
  154.7 3.7 %collective-permute-start.40 = (f32[2,64,512]{2,1,0:T(8,128)S(1)}, f32[2,64,512]{2,1,0:T(8,128)S(1)}, u32[]{:S(2)}, u32[]{:S(2)}) collective-permute-start(f32[2,64,512]{2,1,0:T(8,128)S(1)} %get-tuple-element.154.refs_0_), channel_id=1, source_target_pairs={{0,6},{1,7},{2,0},{3,1},{4,2},{5,3},{6,4},{7,5},{8,14},{9,15},{10,... | collective-permute-start | bytes 786440 | tf_op jit(solution)/shard_map/ppermute | solution.py:302
  158.4 4.1 %collective-permute-done.42.refs_1_.refs_4_ = f32[2,64,512]{2,1,0:T(8,128)S(1)} collective-permute-done((f32[2,64,512]{2,1,0:T(8,128)S(1)}, f32[2,64,512]{2,1,0:T(8,128)S(1)}, u32[]{:S(2)}, u32[]{:S(2)}) %collective-permute-start.42) | collective-permute-done | bytes 262176 | tf_op jit(solution)/shard_map/ppermute | solution.py:298
  170.0 5.6 %collective-permute-done.43.refs_0_.refs_2_ = f32[2,64,512]{2,1,0:T(8,128)S(1)} collective-permute-done((f32[2,64,512]{2,1,0:T(8,128)S(1)}, f32[2,64,512]{2,1,0:T(8,128)S(1)}, u32[]{:S(2)}, u32[]{:S(2)}) %collective-permute-start.43) | collective-permute-done | bytes 262176 | tf_op jit(solution)/shard_map/ppermute | solution.py:302
  180.7 4.6 %inner_rows.15 = (bf16[7,192,512]{2,1,0:T(8,128)(2,1)S(1)}, bf16[7,192,512]{2,1,0:T(8,128)(2,1)S(1)}, f32[1,128]{1,0:T(1,128)}) custom-call(s32[21]{0:T(128)S(1)} %concatenate.6.info, f32[2,64,512]{2,1,0:T(8,128)S(1)} %collective-permute-done.43.refs_0_.refs_2_, f32[2,64,512]{2,1,0:T(8,128)S(1)} %collective-permute-done.46.refs_1_.refs_7_, ...), custom_call_target="tpu_custom_call" | custom-call | flops 2113929216 | tf_op jit(solution)/shard_map/inner_rows/pallas_call | solution.py:30
  185.3 6.9 %middle.5 = (bf16[7,512,512]{2,1,0:T(8,128)(2,1)S(1)}, bf16[7,512,512]{2,1,0:T(8,128)(2,1)S(1)}, f32[2,64,512]{2,1,0:T(8,128)S(1)}, f32[2,64,512]{2,1,0:T(8,128)S(1)}, f32[2,64,512]{2,1,0:T(8,128)S(1)}) custom-call(s32[21]{0:T(128)S(1)} %concatenate.6.info, f32[2,64,512]{2,1,0:T(8,128)S(1)} %collective-permute-done.45.refs_0_.refs_6_, ...), custom_call_target="tpu_custom_call" | custom-call | flops 2818572288 | tf_op jit(solution)/shard_map/middle/pallas_call | solution.py:30
  192.3 5.6 %tail.5 = (f32[8,128]{1,0:T(8,128)S(1)}, f32[2,64,512]{2,1,0:T(8,128)S(1)}, f32[2,64,512]{2,1,0:T(8,128)S(1)}, f32[2,64,512]{2,1,0:T(8,128)S(1)}, f32[2,64,512]{2,1,0:T(8,128)S(1)}, /*index=5*/f32[2,64,512]{2,1,0:T(8,128)S(1)}) custom-call(s32[21]{0:T(128)S(1)} %concatenate.6.info, f32[2,64,512]{2,1,0:T(8,128)S(1)} %get-tuple-element.154.refs_0_, ...), custom_call_target="tpu_custom_call" | custom-call | tf_op jit(solution)/shard_map/tail/pallas_call | solution.py:30
  204.4 8.4 %collective-permute-done.47 = f32[2,64,512]{2,1,0:T(8,128)S(1)} collective-permute-done((f32[2,64,512]{2,1,0:T(8,128)S(1)}, f32[2,64,512]{2,1,0:T(8,128)S(1)}, u32[]{:S(2)}, u32[]{:S(2)}) %collective-permute-start.47) | collective-permute-done | bytes 262176 | tf_op jit(solution)/shard_map/ppermute | solution.py:298
  217.5 8.2 %collective-permute-done.56.refs_5_ = f32[8,128]{1,0:T(8,128)S(1)} collective-permute-done((f32[8,128]{1,0:T(8,128)S(1)}, f32[8,128]{1,0:T(8,128)S(1)}, u32[]{:S(2)}, u32[]{:S(2)}) %collective-permute-start.56) | collective-permute-done | bytes 4128 | tf_op jit(solution)/shard_map/ppermute | solution.py:302
  (163 shorter events, 100.6 us)
Async XLA Ops:
  8.2 13.9 %collective-permute-start = (f32[2,64,512]{2,1,0:T(8,128)S(1)}, f32[2,64,512]{2,1,0:T(8,128)S(1)}, u32[]{:S(2)}, u32[]{:S(2)}) collective-permute-start(f32[2,64,512]{2,1,0:T(8,128)S(1)} %get-tuple-element.95.refs_0_), channel_id=1, source_target_pairs={{0,6},{1,7},{2,0},{3,1},{4,2},{5,3},{6,4},{7,5},{8,14},{9,15},{10,... | collective-permute-start | bytes 786440 | tf_op jit(solution)/shard_map/ppermute | solution.py:302
  17.7 18.0 %collective-permute-start.6 = (f32[2,64,512]{2,1,0:T(8,128)S(1)}, f32[2,64,512]{2,1,0:T(8,128)S(1)}, u32[]{:S(2)}, u32[]{:S(2)}) collective-permute-start(f32[2,64,512]{2,1,0:T(8,128)S(1)} %collective-permute-done.1.refs_0_.refs_2_.refs_3_), channel_id=1, source_target_pairs={{0,1},{1,0},{2,3},{3,2},{4,5},{5,4},{6,7},{7,6},{8,9},{9,8},{10,11... | collective-permute-start | bytes 786440 | tf_op jit(solution)/shard_map/ppermute | solution.py:298
  22.1 13.6 %collective-permute-start.4 = (f32[2,64,512]{2,1,0:T(8,128)S(1)}, f32[2,64,512]{2,1,0:T(8,128)S(1)}, u32[]{:S(2)}, u32[]{:S(2)}) collective-permute-start(f32[2,64,512]{2,1,0:T(8,128)S(1)} %collective-permute-done.refs_1_.refs_3_), channel_id=1, source_target_pairs={{0,1},{1,0},{2,3},{3,2},{4,5},{5,4},{6,7},{7,6},{8,9},{9,8},{10,11... | collective-permute-start | bytes 786440 | tf_op jit(solution)/shard_map/ppermute | solution.py:298
  27.5 12.7 %collective-permute-start.5 = (f32[2,64,512]{2,1,0:T(8,128)S(1)}, f32[2,64,512]{2,1,0:T(8,128)S(1)}, u32[]{:S(2)}, u32[]{:S(2)}) collective-permute-start(f32[2,64,512]{2,1,0:T(8,128)S(1)} %collective-permute-done.3.refs_0_.refs_2_), channel_id=1, source_target_pairs={{0,1},{1,0},{2,3},{3,2},{4,5},{5,4},{6,7},{7,6},{8,9},{9,8},{10,11... | collective-permute-start | bytes 786440 | tf_op jit(solution)/shard_map/ppermute | solution.py:298
  57.8 12.2 %collective-permute-start.17 = (f32[2,64,512]{2,1,0:T(8,128)S(1)}, f32[2,64,512]{2,1,0:T(8,128)S(1)}, u32[]{:S(2)}, u32[]{:S(2)}) collective-permute-start(f32[2,64,512]{2,1,0:T(8,128)S(1)} %get-tuple-element.122), channel_id=1, source_target_pairs={{0,1},{1,0},{2,3},{3,2},{4,5},{5,4},{6,7},{7,6},{8,9},{9,8},{10,11... | collective-permute-start | bytes 786440 | tf_op jit(solution)/shard_map/ppermute | solution.py:298
  66.1 14.9 %collective-permute-start.19 = (f32[2,64,512]{2,1,0:T(8,128)S(1)}, f32[2,64,512]{2,1,0:T(8,128)S(1)}, u32[]{:S(2)}, u32[]{:S(2)}) collective-permute-start(f32[2,64,512]{2,1,0:T(8,128)S(1)} %add.84), channel_id=1, source_target_pairs={{0,6},{1,7},{2,0},{3,1},{4,2},{5,3},{6,4},{7,5},{8,14},{9,15},{10,... | collective-permute-start | bytes 786440 | tf_op jit(solution)/shard_map/ppermute | solution.py:302
  66.1 14.8 %collective-permute-start.18 = (f32[2,64,512]{2,1,0:T(8,128)S(1)}, f32[2,64,512]{2,1,0:T(8,128)S(1)}, u32[]{:S(2)}, u32[]{:S(2)}) collective-permute-start(f32[2,64,512]{2,1,0:T(8,128)S(1)} %add_add_fusion.2), channel_id=1, source_target_pairs={{0,2},{1,3},{2,4},{3,5},{4,6},{5,7},{6,0},{7,1},{8,10},{9,11},{10,... | collective-permute-start | bytes 786440 | tf_op jit(solution)/shard_map/ppermute | solution.py:302
  68.1 12.8 %collective-permute-start.16 = (f32[8,128]{1,0:T(8,128)S(1)}, f32[8,128]{1,0:T(8,128)S(1)}, u32[]{:S(2)}, u32[]{:S(2)}) collective-permute-start(f32[8,128]{1,0:T(8,128)S(1)} %add.90.refs_2_), channel_id=1, source_target_pairs={{0,6},{1,7},{2,0},{3,1},{4,2},{5,3},{6,4},{7,5},{8,14},{9,15},{10,... | collective-permute-start | bytes 12296 | tf_op jit(solution)/shard_map/ppermute | solution.py:302
  82.1 14.0 %collective-permute-start.20 = (f32[2,64,512]{2,1,0:T(8,128)S(1)}, f32[2,64,512]{2,1,0:T(8,128)S(1)}, u32[]{:S(2)}, u32[]{:S(2)}) collective-permute-start(f32[2,64,512]{2,1,0:T(8,128)S(1)} %get-tuple-element.125.refs_0_), channel_id=1, source_target_pairs={{0,6},{1,7},{2,0},{3,1},{4,2},{5,3},{6,4},{7,5},{8,14},{9,15},{10,... | collective-permute-start | bytes 786440 | tf_op jit(solution)/shard_map/ppermute | solution.py:302
  93.5 14.8 %collective-permute-start.26 = (f32[2,64,512]{2,1,0:T(8,128)S(1)}, f32[2,64,512]{2,1,0:T(8,128)S(1)}, u32[]{:S(2)}, u32[]{:S(2)}) collective-permute-start(f32[2,64,512]{2,1,0:T(8,128)S(1)} %collective-permute-done.21.refs_0_.refs_3_), channel_id=1, source_target_pairs={{0,1},{1,0},{2,3},{3,2},{4,5},{5,4},{6,7},{7,6},{8,9},{9,8},{10,11... | collective-permute-start | bytes 786440 | tf_op jit(solution)/shard_map/ppermute | solution.py:298
  96.1 12.2 %collective-permute-start.24 = (f32[2,64,512]{2,1,0:T(8,128)S(1)}, f32[2,64,512]{2,1,0:T(8,128)S(1)}, u32[]{:S(2)}, u32[]{:S(2)}) collective-permute-start(f32[2,64,512]{2,1,0:T(8,128)S(1)} %collective-permute-done.20.refs_1_), channel_id=1, source_target_pairs={{0,1},{1,0},{2,3},{3,2},{4,5},{5,4},{6,7},{7,6},{8,9},{9,8},{10,11... | collective-permute-start | bytes 786440 | tf_op jit(solution)/shard_map/ppermute | solution.py:298
  126.7 13.6 %collective-permute-start.28 = (f32[2,64,512]{2,1,0:T(8,128)S(1)}, f32[2,64,512]{2,1,0:T(8,128)S(1)}, u32[]{:S(2)}, u32[]{:S(2)}) collective-permute-start(f32[2,64,512]{2,1,0:T(8,128)S(1)} %get-tuple-element.137.refs_9_), channel_id=1, source_target_pairs={{0,1},{1,0},{2,3},{3,2},{4,5},{5,4},{6,7},{7,6},{8,9},{9,8},{10,11... | collective-permute-start | bytes 786440 | tf_op jit(solution)/shard_map/ppermute | solution.py:298
  127.4 12.8 %collective-permute-start.27 = (f32[2,64,512]{2,1,0:T(8,128)S(1)}, f32[2,64,512]{2,1,0:T(8,128)S(1)}, u32[]{:S(2)}, u32[]{:S(2)}) collective-permute-start(f32[2,64,512]{2,1,0:T(8,128)S(1)} %get-tuple-element.143), channel_id=1, source_target_pairs={{0,1},{1,0},{2,3},{3,2},{4,5},{5,4},{6,7},{7,6},{8,9},{9,8},{10,11... | collective-permute-start | bytes 786440 | tf_op jit(solution)/shard_map/ppermute | solution.py:298
  130.5 13.8 %collective-permute-start.37 = (f32[2,64,512]{2,1,0:T(8,128)S(1)}, f32[2,64,512]{2,1,0:T(8,128)S(1)}, u32[]{:S(2)}, u32[]{:S(2)}) collective-permute-start(f32[2,64,512]{2,1,0:T(8,128)S(1)} %get-tuple-element.151), channel_id=1, source_target_pairs={{0,1},{1,0},{2,3},{3,2},{4,5},{5,4},{6,7},{7,6},{8,9},{9,8},{10,11... | collective-permute-start | bytes 786440 | tf_op jit(solution)/shard_map/ppermute | solution.py:298
  140.3 12.9 %collective-permute-start.39 = (f32[2,64,512]{2,1,0:T(8,128)S(1)}, f32[2,64,512]{2,1,0:T(8,128)S(1)}, u32[]{:S(2)}, u32[]{:S(2)}) collective-permute-start(f32[2,64,512]{2,1,0:T(8,128)S(1)} %add.91), channel_id=1, source_target_pairs={{0,6},{1,7},{2,0},{3,1},{4,2},{5,3},{6,4},{7,5},{8,14},{9,15},{10,... | collective-permute-start | bytes 786440 | tf_op jit(solution)/shard_map/ppermute | solution.py:302
  140.4 12.8 %collective-permute-start.38 = (f32[2,64,512]{2,1,0:T(8,128)S(1)}, f32[2,64,512]{2,1,0:T(8,128)S(1)}, u32[]{:S(2)}, u32[]{:S(2)}) collective-permute-start(f32[2,64,512]{2,1,0:T(8,128)S(1)} %add_add_fusion.1), channel_id=1, source_target_pairs={{0,2},{1,3},{2,4},{3,5},{4,6},{5,7},{6,0},{7,1},{8,10},{9,11},{10,... | collective-permute-start | bytes 786440 | tf_op jit(solution)/shard_map/ppermute | solution.py:302
  154.7 13.7 %collective-permute-start.40 = (f32[2,64,512]{2,1,0:T(8,128)S(1)}, f32[2,64,512]{2,1,0:T(8,128)S(1)}, u32[]{:S(2)}, u32[]{:S(2)}) collective-permute-start(f32[2,64,512]{2,1,0:T(8,128)S(1)} %get-tuple-element.154.refs_0_), channel_id=1, source_target_pairs={{0,6},{1,7},{2,0},{3,1},{4,2},{5,3},{6,4},{7,5},{8,14},{9,15},{10,... | collective-permute-start | bytes 786440 | tf_op jit(solution)/shard_map/ppermute | solution.py:302
  165.8 14.8 %collective-permute-start.46 = (f32[2,64,512]{2,1,0:T(8,128)S(1)}, f32[2,64,512]{2,1,0:T(8,128)S(1)}, u32[]{:S(2)}, u32[]{:S(2)}) collective-permute-start(f32[2,64,512]{2,1,0:T(8,128)S(1)} %collective-permute-done.41.refs_0_.refs_3_), channel_id=1, source_target_pairs={{0,1},{1,0},{2,3},{3,2},{4,5},{5,4},{6,7},{7,6},{8,9},{9,8},{10,11... | collective-permute-start | bytes 786440 | tf_op jit(solution)/shard_map/ppermute | solution.py:298
  168.3 12.4 %collective-permute-start.44 = (f32[2,64,512]{2,1,0:T(8,128)S(1)}, f32[2,64,512]{2,1,0:T(8,128)S(1)}, u32[]{:S(2)}, u32[]{:S(2)}) collective-permute-start(f32[2,64,512]{2,1,0:T(8,128)S(1)} %collective-permute-done.40.refs_1_), channel_id=1, source_target_pairs={{0,1},{1,0},{2,3},{3,2},{4,5},{5,4},{6,7},{7,6},{8,9},{9,8},{10,11... | collective-permute-start | bytes 786440 | tf_op jit(solution)/shard_map/ppermute | solution.py:298
  199.3 13.6 %collective-permute-start.48 = (f32[2,64,512]{2,1,0:T(8,128)S(1)}, f32[2,64,512]{2,1,0:T(8,128)S(1)}, u32[]{:S(2)}, u32[]{:S(2)}) collective-permute-start(f32[2,64,512]{2,1,0:T(8,128)S(1)} %get-tuple-element.166.refs_9_), channel_id=1, source_target_pairs={{0,1},{1,0},{2,3},{3,2},{4,5},{5,4},{6,7},{7,6},{8,9},{9,8},{10,11... | collective-permute-start | bytes 786440 | tf_op jit(solution)/shard_map/ppermute | solution.py:298
  200.1 12.8 %collective-permute-start.47 = (f32[2,64,512]{2,1,0:T(8,128)S(1)}, f32[2,64,512]{2,1,0:T(8,128)S(1)}, u32[]{:S(2)}, u32[]{:S(2)}) collective-permute-start(f32[2,64,512]{2,1,0:T(8,128)S(1)} %get-tuple-element.172), channel_id=1, source_target_pairs={{0,1},{1,0},{2,3},{3,2},{4,5},{5,4},{6,7},{7,6},{8,9},{9,8},{10,11... | collective-permute-start | bytes 786440 | tf_op jit(solution)/shard_map/ppermute | solution.py:298
  203.1 13.8 %collective-permute-start.57 = (f32[2,64,512]{2,1,0:T(8,128)S(1)}, f32[2,64,512]{2,1,0:T(8,128)S(1)}, u32[]{:S(2)}, u32[]{:S(2)}) collective-permute-start(f32[2,64,512]{2,1,0:T(8,128)S(1)} %get-tuple-element.180), channel_id=1, source_target_pairs={{0,1},{1,0},{2,3},{3,2},{4,5},{5,4},{6,7},{7,6},{8,9},{9,8},{10,11... | collective-permute-start | bytes 786440 | tf_op jit(solution)/shard_map/ppermute | solution.py:298
  213.0 12.7 %collective-permute-start.59 = (f32[2,64,512]{2,1,0:T(8,128)S(1)}, f32[2,64,512]{2,1,0:T(8,128)S(1)}, u32[]{:S(2)}, u32[]{:S(2)}) collective-permute-start(f32[2,64,512]{2,1,0:T(8,128)S(1)} %add.98), channel_id=1, source_target_pairs={{0,6},{1,7},{2,0},{3,1},{4,2},{5,3},{6,4},{7,5},{8,14},{9,15},{10,... | collective-permute-start | bytes 786440 | tf_op jit(solution)/shard_map/ppermute | solution.py:302
  213.1 12.7 %collective-permute-start.58 = (f32[2,64,512]{2,1,0:T(8,128)S(1)}, f32[2,64,512]{2,1,0:T(8,128)S(1)}, u32[]{:S(2)}, u32[]{:S(2)}) collective-permute-start(f32[2,64,512]{2,1,0:T(8,128)S(1)} %add_add_fusion), channel_id=1, source_target_pairs={{0,2},{1,3},{2,4},{3,5},{4,6},{5,7},{6,0},{7,1},{8,10},{9,11},{10,... | collective-permute-start | bytes 786440 | tf_op jit(solution)/shard_map/ppermute | solution.py:302
  (46 other events, 380.2 us)
where the time goes:
time: 240 us; the launch traced here: 245 us
  waiting for transfers between devices  104 us (43%)
  Pallas kernels  75.3 us (31%)
  starting transfers between devices  55.6 us (23%)
  local copies, waits for them, and re-layouts  5.11 us (2%)
  between operations  2.55 us (1%)
  other arithmetic  2.42 us (1%)
    pallas_call x18, Pallas kernels, call(): pl.pallas_call(kernel, in_specs=[pl.BlockSpec(memory_space=pltpu.SMEM)] +...  71.9 us
    ppermute x27, waiting for transfers between devices, around(): lax.ppermute(value, 'term', [(i, (i + 2 * shift) % terms) for i in range(...  49.7 us
    ppermute x24, waiting for transfers between devices, across(): return lax.ppermute(value, 'term', [(i, i ^ 1) for i in range(terms)])  34.6 us
    ppermute x27, starting transfers between devices, around(): lax.ppermute(value, 'term', [(i, (i + 2 * shift) % terms) for i in range(...  25.3 us
    ppermute x24, starting transfers between devices, across(): return lax.ppermute(value, 'term', [(i, i ^ 1) for i in range(terms)])  25.2 us
    ppermute x14, waiting for transfers between devices, stage_sum(): lax.ppermute(values, axis, [(i, i ^ step) for i in range(size)])  19.6 us
    ppermute x14, starting transfers between devices, stage_sum(): lax.ppermute(values, axis, [(i, i ^ step) for i in range(size)])  5.03 us
  transfers between devices with their start and end apart: 65, of which 28 were waited for; matrix products, arithmetic and copies ran while one was open for 0% of the time, Pallas kernels for 21%

commit v1 on v0

--- a/solution.py
+++ b/solution.py
@@ -9,6 +9,7 @@
 
 STEPS = 3
 VMEM_LIMIT = 14 * 1024 * 1024
+SPLIT_VMEM_LIMIT = 42 * 1024 * 1024
 F32 = jnp.float32
 BF16 = jnp.bfloat16
 
@@ -71,7 +72,7 @@
             out_specs=[pl.BlockSpec(memory_space=pltpu.VMEM)] * 2,
         ),
         out_shape=[pltpu.VMEM((slots - 1, width, width), BF16)] * 2,
-        compiler_params=pltpu.CompilerParams(vmem_limit_bytes=VMEM_LIMIT),
+        compiler_params=pltpu.CompilerParams(vmem_limit_bytes=SPLIT_VMEM_LIMIT),
         cost_estimate=pl.CostEstimate(
             flops=0, bytes_accessed=slots * width * width * 4, transcendentals=0
         ),
@@ -142,14 +143,15 @@
         out[target] += product[i * share : (i + 1) * share]
 
 
-def middle_kernel(at, ring, last, groups, order, head, info, *refs):
-    block, parts, refs = refs[0], refs[1 : 1 + 2 * len(groups)], refs[1 + 2 * len(groups) :]
+def middle_kernel(at, ring, lasts, groups, order, head, info, *refs):
+    blocks, refs = refs[: len(lasts)], refs[len(lasts) :]
+    parts, refs = refs[: 2 * len(groups)], refs[2 * len(groups) :]
     right_high, right_low, left_high, left_low = refs[:4]
     full_high, full_low = refs[4:6]
     outs, (high, low) = refs[6:-2], refs[-2:]
-    share = block.shape[1]
+    share = blocks[0].shape[1]
     side = info[at.side]
-    split_blocks([block], high, low)
+    split_blocks(blocks, high, low)
     for out in outs:
         out[...] = jnp.zeros_like(out)
     places = [(r, 1 - side) for r in order[: head[0]]] + [(r, side) for r in order[: head[1]]]
@@ -165,7 +167,8 @@
             for g, group in enumerate(groups):
                 for i, (r, other) in enumerate(group):
                     put(out, k, r, other, parts[2 * g + which][k, i * share : (i + 1) * share, :])
-            put(out, k, last, True, inner[which])
+            for i, r in enumerate(lasts):
+                put(out, k, r, True, inner[which][i * share : (i + 1) * share])
         outer_rows(
             at, info, k, ring, places, (left_high, left_low), (full_high, full_low), outs
         )
@@ -174,18 +177,18 @@
     lax.fori_loop(0, info[at.count], one, 0)
 
 
-def middle(at, info, ring, last, groups, order, head, block, parts, right, left):
+def middle(at, info, ring, lasts, groups, order, head, blocks, parts, right, left):
     live, width, _ = right[0].shape
-    sectors, share, _ = block.shape
+    sectors, share, _ = blocks[0].shape
     count = sum(head)
     results = call(
-        functools.partial(middle_kernel, at, ring, last, groups, order, head),
+        functools.partial(middle_kernel, at, ring, lasts, groups, order, head),
         "middle",
         info,
-        [block, *(array for part in parts for array in part), *right, *left],
-        [((live, width, width), BF16)] * 2 + [(block.shape, F32)] * count,
-        live * share * (1 + count) * width * width * 6,
-        [pltpu.VMEM((sectors, share, width), BF16)] * 2,
+        [*blocks, *(array for part in parts for array in part), *right, *left],
+        [((live, width, width), BF16)] * 2 + [(blocks[0].shape, F32)] * count,
+        live * share * (len(lasts) + count) * width * width * 6,
+        [pltpu.VMEM((sectors, len(lasts) * share, width), BF16)] * 2,
     )
     return results[:2], results[2 : 2 + head[0]], results[2 + head[0] :]
 
@@ -319,9 +322,9 @@
     downs = ring - 1 - ups
     order = []
     for hop in range(ups, 0, -1):
-        order.append(hop)
         if hop <= downs:
             order.append((ring - hop) % ring)
+        order.append(hop)
     return order + [0]
 
 
@@ -343,8 +346,7 @@
         if hop <= downs:
             back = (ring - hop) % ring
             value = own[back] + received[back]
-            value, sums = lax.optimization_barrier((value if down is None else value + down, sums))
-            down = around(value, terms, -1)
+            down = around(value if down is None else value + down, terms, -1)
     parts = [sums] + [around(sums, terms, shift) for shift in range(1, ring)]
     return [term for term in (own[0], received[0], up, down) if term is not None], parts
 
@@ -369,7 +371,7 @@
     ups = ring // 2
     downs = ring - 1 - ups
     last = ring - ups
-    head = (ring // 2, ring // 4)
+    head = (1, 0)
     right = left = None
     for step in range(STEPS):
         mine, theirs, groups, parts = {0: vector}, {}, [], []
@@ -415,14 +417,15 @@
         fresh = [last] + ([ups] if ups <= downs else [])
         for r in fresh:
             theirs[r] = across(mine[r], terms)
-        group = [(r, False) for r in fresh] + before + [(r, True) for r in fresh if r != last]
+        lasts = [r for r, _ in before[1:]] + fresh
+        group = [(r, False) for r in fresh] + before[:1]
         *part, token = inner_rows(
             at, info, [(theirs if other else mine)[r] for r, other in group], right, (token,)
         )
         groups.append(group)
         parts.append(part)
         full, others, owns = middle(
-            at, info, ring, last, groups, order, head, theirs[last], parts, right, left
+            at, info, ring, lasts, groups, order, head, [theirs[r] for r in lasts], parts, right, left
         )
         sums, more_others, more_owns = tail(
             at,

time: 240 us -> 241 us (level); the launches traced: 245 us -> 243 us
  waiting for transfers between devices: 104 us -> 91 us
  Pallas kernels: 75.3 us -> 84.5 us
  starting transfers between devices: 55.6 us -> 60.7 us
  local copies, waits for them, and re-layouts: 5.11 us -> 1.72 us
    ppermute x24, waiting for transfers between devices: 34.6 us -> 24.6 us  [across(): return lax.ppermute(value, 'term', [(i, i ^ 1) for i in range(terms)])]
    pallas_call x2, Pallas kernels: 3.41 us -> 12.4 us  [split_operators(): pl.pallas_call(functools.partial(split_kernel, at), grid_spec=pltpu.Prefe...]
    ppermute x27, starting transfers between devices: 25.3 us -> 33.1 us  [around(): lax.ppermute(value, 'term', [(i, (i + 2 * shift) % terms) for i in range(...]
    ppermute x27, waiting for transfers between devices: 49.7 us -> 45.6 us  [around(): lax.ppermute(value, 'term', [(i, (i + 2 * shift) % terms) for i in range(...]
    unnamed x10 -> x4, local copies, waits for them, and re-layouts: 4.35 us -> 0.96 us
  transfers between devices with their start and end apart: 65 -> 65, of which waited for: 28 -> 35; matrix products, arithmetic and copies ran while one was open for 0% -> 0% of each run, Pallas kernels for 21% -> 26%
where the time goes in v1:
time: 241 us; the launch traced here: 243 us
  waiting for transfers between devices  91 us (38%)
  Pallas kernels  84.5 us (35%)
  starting transfers between devices  60.7 us (25%)
  between operations  2.43 us (1%)
    pallas_call x18, Pallas kernels, call(): pl.pallas_call(kernel, in_specs=[pl.BlockSpec(memory_space=pltpu.SMEM)] +...  72.1 us
    ppermute x27, waiting for transfers between devices, around(): lax.ppermute(value, 'term', [(i, (i + 2 * shift) % terms) for i in range(...  45.6 us
    ppermute x27, starting transfers between devices, around(): lax.ppermute(value, 'term', [(i, (i + 2 * shift) % terms) for i in range(...  33.1 us
    ppermute x24, waiting for transfers between devices, across(): return lax.ppermute(value, 'term', [(i, i ^ 1) for i in range(terms)])  24.6 us
    ppermute x24, starting transfers between devices, across(): return lax.ppermute(value, 'term', [(i, i ^ 1) for i in range(terms)])  23.9 us
    ppermute x14, waiting for transfers between devices, stage_sum(): lax.ppermute(values, axis, [(i, i ^ step) for i in range(size)])  20.8 us
    pallas_call x2, Pallas kernels, split_operators(): pl.pallas_call(functools.partial(split_kernel, at), grid_spec=pltpu.Prefe...  12.4 us
  transfers between devices with their start and end apart: 65, of which 35 were waited for; matrix products, arithmetic and copies ran while one was open for 0% of the time, Pallas kernels for 26%

profile of v1, /device:TPU:0, one launch (start us, length us, event | category | flops | bytes accessed | tf_op | source)
XLA Modules:
  0.0 242.8 jit_solution(13373165819143260522)
XLA Ops:
  12.9 4.8 %collective-permute-done.1.refs_0_.refs_2_.refs_3_ = f32[2,64,512]{2,1,0:T(8,128)S(1)} collective-permute-done((f32[2,64,512]{2,1,0:T(8,128)S(1)}, f32[2,64,512]{2,1,0:T(8,128)S(1)}, u32[]{:S(2)}, u32[]{:S(2)}) %collective-permute-start.1) | collective-permute-done | bytes 262176 | tf_op jit(solution)/shard_map/ppermute | solution.py:305
  18.0 4.1 %collective-permute-done.refs_1_.refs_3_ = f32[2,64,512]{2,1,0:T(8,128)S(1)} collective-permute-done((f32[2,64,512]{2,1,0:T(8,128)S(1)}, f32[2,64,512]{2,1,0:T(8,128)S(1)}, u32[]{:S(2)}, u32[]{:S(2)}) %collective-permute-start) | collective-permute-done | bytes 262176 | tf_op jit(solution)/shard_map/ppermute | solution.py:305
  22.4 6.2 %split_right.1 = (bf16[7,512,512]{2,1,0:T(8,128)(2,1)S(1)}, bf16[7,512,512]{2,1,0:T(8,128)(2,1)S(1)}) custom-call(s32[21]{0:T(128)S(1)} %concatenate.6.info, f32[8,512,512]{2,1,0:T(8,128)} %operator.2, f32[2,64,512]{2,1,0:T(8,128)S(1)} %collective-permute-done.1.refs_0_.refs_2_.refs_3_, f32[2,64,512]{2,1,0:T(8,128)S(1)} %collective-permute-done.refs_1_.refs_3_), custom_call_target="tpu_custom_call" | custom-call | bytes 8388608 | tf_op jit(solution)/shard_map/split_right/pallas_call | solution.py:61
  29.0 4.7 %inner_rows.8 = (bf16[7,256,512]{2,1,0:T(8,128)(2,1)S(1)}, bf16[7,256,512]{2,1,0:T(8,128)(2,1)S(1)}, f32[1,128]{1,0:T(1,128)S(1)}) custom-call(s32[21]{0:T(128)S(1)} %concatenate.6.info, f32[2,64,512]{2,1,0:T(8,128)S(1)} %get-tuple-element.89.refs_0_, f32[2,64,512]{2,1,0:T(8,128)S(1)} %collective-permute-done.2.refs_1_.refs_4_, ...), custom_call_target="tpu_custom_call" | custom-call | flops 2818572288 | tf_op jit(solution)/shard_map/inner_rows/pallas_call | solution.py:31
  33.8 6.2 %split_left.1 = (bf16[7,512,512]{2,1,0:T(8,128)(2,1)S(1)}, bf16[7,512,512]{2,1,0:T(8,128)(2,1)S(1)}) custom-call(s32[21]{0:T(128)S(1)} %concatenate.6.info, f32[8,512,512]{2,1,0:T(8,128)} %operator.3, f32[2,64,512]{2,1,0:T(8,128)S(1)} %collective-permute-done.1.refs_0_.refs_2_.refs_3_, f32[2,64,512]{2,1,0:T(8,128)S(1)} %collective-permute-done.refs_1_.refs_3_), custom_call_target="tpu_custom_call" | custom-call | bytes 8388608 | tf_op jit(solution)/shard_map/split_left/pallas_call | solution.py:61
  40.0 3.8 %inner_rows.9 = (bf16[7,128,512]{2,1,0:T(8,128)(2,1)S(1)}, bf16[7,128,512]{2,1,0:T(8,128)(2,1)S(1)}, f32[1,128]{1,0:T(1,128)}) custom-call(s32[21]{0:T(128)S(1)} %concatenate.6.info, f32[2,64,512]{2,1,0:T(8,128)S(1)} %collective-permute-done.3.refs_0_.refs_2_, f32[2,64,512]{2,1,0:T(8,128)S(1)} %collective-permute-done.6.refs_1_.refs_7_, ...), custom_call_target="tpu_custom_call" | custom-call | flops 1409286144 | tf_op jit(solution)/shard_map/inner_rows/pallas_call | solution.py:31
  43.8 6.0 %middle.3 = (bf16[7,512,512]{2,1,0:T(8,128)(2,1)S(1)}, bf16[7,512,512]{2,1,0:T(8,128)(2,1)S(1)}, f32[2,64,512]{2,1,0:T(8,128)S(1)}) custom-call(s32[21]{0:T(128)S(1)} %concatenate.6.info, f32[2,64,512]{2,1,0:T(8,128)S(1)} %collective-permute-done.4.refs_0_.refs_5_, f32[2,64,512]{2,1,0:T(8,128)S(1)} %collective-permute-done.5.refs_1_.refs_6_, ...), custom_call_target="tpu_custom_call" | custom-call | flops 2113929216 | tf_op jit(solution)/shard_map/middle/pallas_call | solution.py:31
  50.0 7.1 %tail.3 = (f32[8,128]{1,0:T(8,128)S(1)}, f32[2,64,512]{2,1,0:T(8,128)S(1)}, f32[2,64,512]{2,1,0:T(8,128)S(1)}, f32[2,64,512]{2,1,0:T(8,128)S(1)}, f32[2,64,512]{...) custom-call(s32[21]{0:T(128)S(1)} %concatenate.6.info, ...), custom_call_target="tpu_custom_call" | custom-call | tf_op jit(solution)/shard_map/tail/pallas_call | solution.py:31
  69.2 6.1 %collective-permute-start.17 = (f32[2,64,512]{2,1,0:T(8,128)S(1)}, f32[2,64,512]{2,1,0:T(8,128)S(1)}, u32[]{:S(2)}, u32[]{:S(2)}) collective-permute-start(f32[2,64,512]{2,1,0:T(8,128)S(1)} %add_add_fusion.2), channel_id=1, source_target_pairs={{0,2},{1,3},{2,4},{3,5},{4,6},{5,7},{6,0},{7,1},{8,10},{9,11},{10,... | collective-permute-start | bytes 786440 | tf_op jit(solution)/shard_map/ppermute | solution.py:305
  75.3 3.5 %collective-permute-start.14 = (f32[8,128]{1,0:T(8,128)S(1)}, f32[8,128]{1,0:T(8,128)S(1)}, u32[]{:S(2)}, u32[]{:S(2)}) collective-permute-start(f32[8,128]{1,0:T(8,128)S(1)} %add.89.refs_2_), channel_id=1, source_target_pairs={{0,4},{1,5},{2,6},{3,7},{4,0},{5,1},{6,2},{7,3},{8,12},{9,13},{10,... | collective-permute-start | bytes 12296 | tf_op jit(solution)/shard_map/ppermute | solution.py:305
  79.0 5.1 %collective-permute-done.19.refs_9_ = f32[2,64,512]{2,1,0:T(8,128)S(1)} collective-permute-done((f32[2,64,512]{2,1,0:T(8,128)S(1)}, f32[2,64,512]{2,1,0:T(8,128)S(1)}, u32[]{:S(2)}, u32[]{:S(2)}) %collective-permute-start.19) | collective-permute-done | bytes 262176 | tf_op jit(solution)/shard_map/ppermute | solution.py:305
  102.4 4.9 %collective-permute-done.23.refs_0_.refs_2_ = f32[2,64,512]{2,1,0:T(8,128)S(1)} collective-permute-done((f32[2,64,512]{2,1,0:T(8,128)S(1)}, f32[2,64,512]{2,1,0:T(8,128)S(1)}, u32[]{:S(2)}, u32[]{:S(2)}) %collective-permute-start.23) | collective-permute-done | bytes 262176 | tf_op jit(solution)/shard_map/ppermute | solution.py:305
  111.7 3.8 %inner_rows.12 = (bf16[7,128,512]{2,1,0:T(8,128)(2,1)S(1)}, bf16[7,128,512]{2,1,0:T(8,128)(2,1)S(1)}, f32[1,128]{1,0:T(1,128)}) custom-call(s32[21]{0:T(128)S(1)} %concatenate.6.info, f32[2,64,512]{2,1,0:T(8,128)S(1)} %collective-permute-done.23.refs_0_.refs_2_, f32[2,64,512]{2,1,0:T(8,128)S(1)} %collective-permute-done.26.refs_1_.refs_7_, ...), custom_call_target="tpu_custom_call" | custom-call | flops 1409286144 | tf_op jit(solution)/shard_map/inner_rows/pallas_call | solution.py:31
  115.6 6.1 %middle.4 = (bf16[7,512,512]{2,1,0:T(8,128)(2,1)S(1)}, bf16[7,512,512]{2,1,0:T(8,128)(2,1)S(1)}, f32[2,64,512]{2,1,0:T(8,128)S(1)}) custom-call(s32[21]{0:T(128)S(1)} %concatenate.6.info, f32[2,64,512]{2,1,0:T(8,128)S(1)} %collective-permute-done.24.refs_0_.refs_5_, f32[2,64,512]{2,1,0:T(8,128)S(1)} %collective-permute-done.25.refs_1_.refs_6_, ...), custom_call_target="tpu_custom_call" | custom-call | flops 2113929216 | tf_op jit(solution)/shard_map/middle/pallas_call | solution.py:31
  121.8 7.1 %tail.4 = (f32[8,128]{1,0:T(8,128)S(1)}, f32[2,64,512]{2,1,0:T(8,128)S(1)}, f32[2,64,512]{2,1,0:T(8,128)S(1)}, f32[2,64,512]{2,1,0:T(8,128)S(1)}, f32[2,64,512]{...) custom-call(s32[21]{0:T(128)S(1)} %concatenate.6.info, ...), custom_call_target="tpu_custom_call" | custom-call | tf_op jit(solution)/shard_map/tail/pallas_call | solution.py:31
  135.1 7.0 %collective-permute-done.38 = f32[2,64,512]{2,1,0:T(8,128)S(1)} collective-permute-done((f32[2,64,512]{2,1,0:T(8,128)S(1)}, f32[2,64,512]{2,1,0:T(8,128)S(1)}, u32[]{:S(2)}, u32[]{:S(2)}) %collective-permute-start.38) | collective-permute-done | bytes 262176 | tf_op jit(solution)/shard_map/ppermute | solution.py:301
  147.9 6.4 %collective-permute-done.39.refs_9_ = f32[2,64,512]{2,1,0:T(8,128)S(1)} collective-permute-done((f32[2,64,512]{2,1,0:T(8,128)S(1)}, f32[2,64,512]{2,1,0:T(8,128)S(1)}, u32[]{:S(2)}, u32[]{:S(2)}) %collective-permute-start.39) | collective-permute-done | bytes 262176 | tf_op jit(solution)/shard_map/ppermute | solution.py:305
  172.1 4.1 %collective-permute-done.43.refs_0_.refs_2_ = f32[2,64,512]{2,1,0:T(8,128)S(1)} collective-permute-done((f32[2,64,512]{2,1,0:T(8,128)S(1)}, f32[2,64,512]{2,1,0:T(8,128)S(1)}, u32[]{:S(2)}, u32[]{:S(2)}) %collective-permute-start.43) | collective-permute-done | bytes 262176 | tf_op jit(solution)/shard_map/ppermute | solution.py:305
  181.4 3.8 %inner_rows.15 = (bf16[7,128,512]{2,1,0:T(8,128)(2,1)S(1)}, bf16[7,128,512]{2,1,0:T(8,128)(2,1)S(1)}, f32[1,128]{1,0:T(1,128)}) custom-call(s32[21]{0:T(128)S(1)} %concatenate.6.info, f32[2,64,512]{2,1,0:T(8,128)S(1)} %collective-permute-done.43.refs_0_.refs_2_, f32[2,64,512]{2,1,0:T(8,128)S(1)} %collective-permute-done.46.refs_1_.refs_7_, ...), custom_call_target="tpu_custom_call" | custom-call | flops 1409286144 | tf_op jit(solution)/shard_map/inner_rows/pallas_call | solution.py:31
  185.3 6.1 %middle.5 = (bf16[7,512,512]{2,1,0:T(8,128)(2,1)S(1)}, bf16[7,512,512]{2,1,0:T(8,128)(2,1)S(1)}, f32[2,64,512]{2,1,0:T(8,128)S(1)}) custom-call(s32[21]{0:T(128)S(1)} %concatenate.6.info, f32[2,64,512]{2,1,0:T(8,128)S(1)} %collective-permute-done.44.refs_0_.refs_5_, f32[2,64,512]{2,1,0:T(8,128)S(1)} %collective-permute-done.45.refs_1_.refs_6_, ...), custom_call_target="tpu_custom_call" | custom-call | flops 2113929216 | tf_op jit(solution)/shard_map/middle/pallas_call | solution.py:31
  191.4 7.3 %tail.5 = (f32[8,128]{1,0:T(8,128)S(1)}, f32[2,64,512]{2,1,0:T(8,128)S(1)}, f32[2,64,512]{2,1,0:T(8,128)S(1)}, f32[2,64,512]{2,1,0:T(8,128)S(1)}, f32[2,64,512]{...) custom-call(s32[21]{0:T(128)S(1)} %concatenate.6.info, ...), custom_call_target="tpu_custom_call" | custom-call | tf_op jit(solution)/shard_map/tail/pallas_call | solution.py:31
  204.2 7.0 %collective-permute-done.58 = f32[2,64,512]{2,1,0:T(8,128)S(1)} collective-permute-done((f32[2,64,512]{2,1,0:T(8,128)S(1)}, f32[2,64,512]{2,1,0:T(8,128)S(1)}, u32[]{:S(2)}, u32[]{:S(2)}) %collective-permute-start.58) | collective-permute-done | bytes 262176 | tf_op jit(solution)/shard_map/ppermute | solution.py:301
  216.4 7.0 %collective-permute-done.59.refs_9_ = f32[2,64,512]{2,1,0:T(8,128)S(1)} collective-permute-done((f32[2,64,512]{2,1,0:T(8,128)S(1)}, f32[2,64,512]{2,1,0:T(8,128)S(1)}, u32[]{:S(2)}, u32[]{:S(2)}) %collective-permute-start.59) | collective-permute-done | bytes 262176 | tf_op jit(solution)/shard_map/ppermute | solution.py:305
  236.9 3.8 %collective-permute-done.64 = f32[1,128]{1,0:T(1,128)S(1)} collective-permute-done((f32[1,128]{1,0:T(1,128)S(1)}, f32[1,128]{1,0:T(1,128)S(1)}, u32[]{:S(2)}, u32[]{:S(2)}) %collective-permute-start.64) | collective-permute-done | bytes 544 | tf_op jit(solution)/shard_map/ppermute | solution.py:317
  (156 shorter events, 108.2 us)
Async XLA Ops:
  8.2 13.9 %collective-permute-start = (f32[2,64,512]{2,1,0:T(8,128)S(1)}, f32[2,64,512]{2,1,0:T(8,128)S(1)}, u32[]{:S(2)}, u32[]{:S(2)}) collective-permute-start(f32[2,64,512]{2,1,0:T(8,128)S(1)} %get-tuple-element.89.refs_0_), channel_id=1, source_target_pairs={{0,6},{1,7},{2,0},{3,1},{4,2},{5,3},{6,4},{7,5},{8,14},{9,15},{10,... | collective-permute-start | bytes 786440 | tf_op jit(solution)/shard_map/ppermute | solution.py:305
  17.7 22.3 %collective-permute-start.6 = (f32[2,64,512]{2,1,0:T(8,128)S(1)}, f32[2,64,512]{2,1,0:T(8,128)S(1)}, u32[]{:S(2)}, u32[]{:S(2)}) collective-permute-start(f32[2,64,512]{2,1,0:T(8,128)S(1)} %collective-permute-done.1.refs_0_.refs_2_.refs_3_), channel_id=1, source_target_pairs={{0,1},{1,0},{2,3},{3,2},{4,5},{5,4},{6,7},{7,6},{8,9},{9,8},{10,11... | collective-permute-start | bytes 786440 | tf_op jit(solution)/shard_map/ppermute | solution.py:301
  22.1 21.7 %collective-permute-start.4 = (f32[2,64,512]{2,1,0:T(8,128)S(1)}, f32[2,64,512]{2,1,0:T(8,128)S(1)}, u32[]{:S(2)}, u32[]{:S(2)}) collective-permute-start(f32[2,64,512]{2,1,0:T(8,128)S(1)} %collective-permute-done.refs_1_.refs_3_), channel_id=1, source_target_pairs={{0,1},{1,0},{2,3},{3,2},{4,5},{5,4},{6,7},{7,6},{8,9},{9,8},{10,11... | collective-permute-start | bytes 786440 | tf_op jit(solution)/shard_map/ppermute | solution.py:301
  28.6 15.3 %collective-permute-start.5 = (f32[2,64,512]{2,1,0:T(8,128)S(1)}, f32[2,64,512]{2,1,0:T(8,128)S(1)}, u32[]{:S(2)}, u32[]{:S(2)}) collective-permute-start(f32[2,64,512]{2,1,0:T(8,128)S(1)} %collective-permute-done.3.refs_0_.refs_2_), channel_id=1, source_target_pairs={{0,1},{1,0},{2,3},{3,2},{4,5},{5,4},{6,7},{7,6},{8,9},{9,8},{10,11... | collective-permute-start | bytes 786440 | tf_op jit(solution)/shard_map/ppermute | solution.py:301
  57.3 11.3 %collective-permute-start.7 = (f32[2,64,512]{2,1,0:T(8,128)S(1)}, f32[2,64,512]{2,1,0:T(8,128)S(1)}, u32[]{:S(2)}, u32[]{:S(2)}) collective-permute-start(f32[2,64,512]{2,1,0:T(8,128)S(1)} %get-tuple-element.106), channel_id=1, source_target_pairs={{0,1},{1,0},{2,3},{3,2},{4,5},{5,4},{6,7},{7,6},{8,9},{9,8},{10,11... | collective-permute-start | bytes 786440 | tf_op jit(solution)/shard_map/ppermute | solution.py:301
  63.5 15.3 %collective-permute-start.16 = (f32[2,64,512]{2,1,0:T(8,128)S(1)}, f32[2,64,512]{2,1,0:T(8,128)S(1)}, u32[]{:S(2)}, u32[]{:S(2)}) collective-permute-start(f32[2,64,512]{2,1,0:T(8,128)S(1)} %get-tuple-element.113), channel_id=1, source_target_pairs={{0,1},{1,0},{2,3},{3,2},{4,5},{5,4},{6,7},{7,6},{8,9},{9,8},{10,11... | collective-permute-start | bytes 786440 | tf_op jit(solution)/shard_map/ppermute | solution.py:301
  68.5 15.6 %collective-permute-start.19 = (f32[2,64,512]{2,1,0:T(8,128)S(1)}, f32[2,64,512]{2,1,0:T(8,128)S(1)}, u32[]{:S(2)}, u32[]{:S(2)}) collective-permute-start(f32[2,64,512]{2,1,0:T(8,128)S(1)} %add.90), channel_id=1, source_target_pairs={{0,6},{1,7},{2,0},{3,1},{4,2},{5,3},{6,4},{7,5},{8,14},{9,15},{10,... | collective-permute-start | bytes 786440 | tf_op jit(solution)/shard_map/ppermute | solution.py:305
  69.2 16.4 %collective-permute-start.17 = (f32[2,64,512]{2,1,0:T(8,128)S(1)}, f32[2,64,512]{2,1,0:T(8,128)S(1)}, u32[]{:S(2)}, u32[]{:S(2)}) collective-permute-start(f32[2,64,512]{2,1,0:T(8,128)S(1)} %add_add_fusion.2), channel_id=1, source_target_pairs={{0,2},{1,3},{2,4},{3,5},{4,6},{5,7},{6,0},{7,1},{8,10},{9,11},{10,... | collective-permute-start | bytes 786440 | tf_op jit(solution)/shard_map/ppermute | solution.py:305
  87.7 13.4 %collective-permute-start.20 = (f32[2,64,512]{2,1,0:T(8,128)S(1)}, f32[2,64,512]{2,1,0:T(8,128)S(1)}, u32[]{:S(2)}, u32[]{:S(2)}) collective-permute-start(f32[2,64,512]{2,1,0:T(8,128)S(1)} %get-tuple-element.117.refs_0_), channel_id=1, source_target_pairs={{0,6},{1,7},{2,0},{3,1},{4,2},{5,3},{6,4},{7,5},{8,14},{9,15},{10,... | collective-permute-start | bytes 786440 | tf_op jit(solution)/shard_map/ppermute | solution.py:305
  98.2 13.5 %collective-permute-start.26 = (f32[2,64,512]{2,1,0:T(8,128)S(1)}, f32[2,64,512]{2,1,0:T(8,128)S(1)}, u32[]{:S(2)}, u32[]{:S(2)}) collective-permute-start(f32[2,64,512]{2,1,0:T(8,128)S(1)} %collective-permute-done.21.refs_0_.refs_3_), channel_id=1, source_target_pairs={{0,1},{1,0},{2,3},{3,2},{4,5},{5,4},{6,7},{7,6},{8,9},{9,8},{10,11... | collective-permute-start | bytes 786440 | tf_op jit(solution)/shard_map/ppermute | solution.py:301
  101.1 14.4 %collective-permute-start.24 = (f32[2,64,512]{2,1,0:T(8,128)S(1)}, f32[2,64,512]{2,1,0:T(8,128)S(1)}, u32[]{:S(2)}, u32[]{:S(2)}) collective-permute-start(f32[2,64,512]{2,1,0:T(8,128)S(1)} %collective-permute-done.20.refs_1_), channel_id=1, source_target_pairs={{0,1},{1,0},{2,3},{3,2},{4,5},{5,4},{6,7},{7,6},{8,9},{9,8},{10,11... | collective-permute-start | bytes 786440 | tf_op jit(solution)/shard_map/ppermute | solution.py:301
  129.2 13.0 %collective-permute-start.27 = (f32[2,64,512]{2,1,0:T(8,128)S(1)}, f32[2,64,512]{2,1,0:T(8,128)S(1)}, u32[]{:S(2)}, u32[]{:S(2)}) collective-permute-start(f32[2,64,512]{2,1,0:T(8,128)S(1)} %get-tuple-element.133), channel_id=1, source_target_pairs={{0,1},{1,0},{2,3},{3,2},{4,5},{5,4},{6,7},{7,6},{8,9},{9,8},{10,11... | collective-permute-start | bytes 786440 | tf_op jit(solution)/shard_map/ppermute | solution.py:301
  131.0 11.1 %collective-permute-start.38 = (f32[2,64,512]{2,1,0:T(8,128)S(1)}, f32[2,64,512]{2,1,0:T(8,128)S(1)}, u32[]{:S(2)}, u32[]{:S(2)}) collective-permute-start(f32[2,64,512]{2,1,0:T(8,128)S(1)} %get-tuple-element.143), channel_id=1, source_target_pairs={{0,1},{1,0},{2,3},{3,2},{4,5},{5,4},{6,7},{7,6},{8,9},{9,8},{10,11... | collective-permute-start | bytes 786440 | tf_op jit(solution)/shard_map/ppermute | solution.py:301
  134.0 13.8 %collective-permute-start.36 = (f32[2,64,512]{2,1,0:T(8,128)S(1)}, f32[2,64,512]{2,1,0:T(8,128)S(1)}, u32[]{:S(2)}, u32[]{:S(2)}) collective-permute-start(f32[2,64,512]{2,1,0:T(8,128)S(1)} %get-tuple-element.140), channel_id=1, source_target_pairs={{0,1},{1,0},{2,3},{3,2},{4,5},{5,4},{6,7},{7,6},{8,9},{9,8},{10,11... | collective-permute-start | bytes 786440 | tf_op jit(solution)/shard_map/ppermute | solution.py:301
  142.1 12.2 %collective-permute-start.39 = (f32[2,64,512]{2,1,0:T(8,128)S(1)}, f32[2,64,512]{2,1,0:T(8,128)S(1)}, u32[]{:S(2)}, u32[]{:S(2)}) collective-permute-start(f32[2,64,512]{2,1,0:T(8,128)S(1)} %add.97), channel_id=1, source_target_pairs={{0,6},{1,7},{2,0},{3,1},{4,2},{5,3},{6,4},{7,5},{8,14},{9,15},{10,... | collective-permute-start | bytes 786440 | tf_op jit(solution)/shard_map/ppermute | solution.py:305
  142.3 13.6 %collective-permute-start.37 = (f32[2,64,512]{2,1,0:T(8,128)S(1)}, f32[2,64,512]{2,1,0:T(8,128)S(1)}, u32[]{:S(2)}, u32[]{:S(2)}) collective-permute-start(f32[2,64,512]{2,1,0:T(8,128)S(1)} %add_add_fusion.1), channel_id=1, source_target_pairs={{0,2},{1,3},{2,4},{3,5},{4,6},{5,7},{6,0},{7,1},{8,10},{9,11},{10,... | collective-permute-start | bytes 786440 | tf_op jit(solution)/shard_map/ppermute | solution.py:305
  157.6 12.5 %collective-permute-start.40 = (f32[2,64,512]{2,1,0:T(8,128)S(1)}, f32[2,64,512]{2,1,0:T(8,128)S(1)}, u32[]{:S(2)}, u32[]{:S(2)}) collective-permute-start(f32[2,64,512]{2,1,0:T(8,128)S(1)} %get-tuple-element.144.refs_0_), channel_id=1, source_target_pairs={{0,6},{1,7},{2,0},{3,1},{4,2},{5,3},{6,4},{7,5},{8,14},{9,15},{10,... | collective-permute-start | bytes 786440 | tf_op jit(solution)/shard_map/ppermute | solution.py:305
  168.0 13.4 %collective-permute-start.46 = (f32[2,64,512]{2,1,0:T(8,128)S(1)}, f32[2,64,512]{2,1,0:T(8,128)S(1)}, u32[]{:S(2)}, u32[]{:S(2)}) collective-permute-start(f32[2,64,512]{2,1,0:T(8,128)S(1)} %collective-permute-done.41.refs_0_.refs_3_), channel_id=1, source_target_pairs={{0,1},{1,0},{2,3},{3,2},{4,5},{5,4},{6,7},{7,6},{8,9},{9,8},{10,11... | collective-permute-start | bytes 786440 | tf_op jit(solution)/shard_map/ppermute | solution.py:301
  170.2 15.1 %collective-permute-start.44 = (f32[2,64,512]{2,1,0:T(8,128)S(1)}, f32[2,64,512]{2,1,0:T(8,128)S(1)}, u32[]{:S(2)}, u32[]{:S(2)}) collective-permute-start(f32[2,64,512]{2,1,0:T(8,128)S(1)} %collective-permute-done.40.refs_1_), channel_id=1, source_target_pairs={{0,1},{1,0},{2,3},{3,2},{4,5},{5,4},{6,7},{7,6},{8,9},{9,8},{10,11... | collective-permute-start | bytes 786440 | tf_op jit(solution)/shard_map/ppermute | solution.py:301
  191.4 11.2 %collective-permute-start.48 = (f32[2,64,512]{2,1,0:T(8,128)S(1)}, f32[2,64,512]{2,1,0:T(8,128)S(1)}, u32[]{:S(2)}, u32[]{:S(2)}) collective-permute-start(f32[2,64,512]{2,1,0:T(8,128)S(1)} %get-tuple-element.155.refs_8_), channel_id=1, source_target_pairs={{0,1},{1,0},{2,3},{3,2},{4,5},{5,4},{6,7},{7,6},{8,9},{9,8},{10,11... | collective-permute-start | bytes 786440 | tf_op jit(solution)/shard_map/ppermute | solution.py:301
  199.0 12.3 %collective-permute-start.47 = (f32[2,64,512]{2,1,0:T(8,128)S(1)}, f32[2,64,512]{2,1,0:T(8,128)S(1)}, u32[]{:S(2)}, u32[]{:S(2)}) collective-permute-start(f32[2,64,512]{2,1,0:T(8,128)S(1)} %get-tuple-element.160), channel_id=1, source_target_pairs={{0,1},{1,0},{2,3},{3,2},{4,5},{5,4},{6,7},{7,6},{8,9},{9,8},{10,11... | collective-permute-start | bytes 786440 | tf_op jit(solution)/shard_map/ppermute | solution.py:301
  203.9 11.9 %collective-permute-start.56 = (f32[2,64,512]{2,1,0:T(8,128)S(1)}, f32[2,64,512]{2,1,0:T(8,128)S(1)}, u32[]{:S(2)}, u32[]{:S(2)}) collective-permute-start(f32[2,64,512]{2,1,0:T(8,128)S(1)} %get-tuple-element.167), channel_id=1, source_target_pairs={{0,1},{1,0},{2,3},{3,2},{4,5},{5,4},{6,7},{7,6},{8,9},{9,8},{10,11... | collective-permute-start | bytes 786440 | tf_op jit(solution)/shard_map/ppermute | solution.py:301
  211.2 12.1 %collective-permute-start.59 = (f32[2,64,512]{2,1,0:T(8,128)S(1)}, f32[2,64,512]{2,1,0:T(8,128)S(1)}, u32[]{:S(2)}, u32[]{:S(2)}) collective-permute-start(f32[2,64,512]{2,1,0:T(8,128)S(1)} %add.104), channel_id=1, source_target_pairs={{0,6},{1,7},{2,0},{3,1},{4,2},{5,3},{6,4},{7,5},{8,14},{9,15},{10,... | collective-permute-start | bytes 786440 | tf_op jit(solution)/shard_map/ppermute | solution.py:305
  211.9 11.8 %collective-permute-start.57 = (f32[2,64,512]{2,1,0:T(8,128)S(1)}, f32[2,64,512]{2,1,0:T(8,128)S(1)}, u32[]{:S(2)}, u32[]{:S(2)}) collective-permute-start(f32[2,64,512]{2,1,0:T(8,128)S(1)} %add_add_fusion), channel_id=1, source_target_pairs={{0,2},{1,3},{2,4},{3,5},{4,6},{5,7},{6,0},{7,1},{8,10},{9,11},{10,... | collective-permute-start | bytes 786440 | tf_op jit(solution)/shard_map/ppermute | solution.py:305
  (43 other events, 338.0 us)
